TPU v7x, 32 devices: a whole 2x2x4 slice. The times are simulated.
32 devices in a mesh: section: 2 (over y), node: 4 (over x, core), local: 4 (over z).
Axes of the slice: x: 2, y: 2, z: 4, core: 2. Of those that a mesh axis runs over, the one named last changes fastest.
Arguments:
- tokens: bfloat16 [2, 96, 7168], P(None, ('section', 'node', 'local')), may hold values from -6 to 6
- norm_gain: float32 [7168], replicated, may hold values from 0.1 to 1.9
- routes: int32 [2, 96, 2], P(None, ('section', 'node', 'local')), may hold values from 0 to 3, all different within a row; in each aligned block of 3 rows (0 to 2, 3 to 5, ..., all dimensions but the last counted through in order) at most 2 rows name the same one
- gate_weight: float32 [2, 96, 2], P(None, ('section', 'node', 'local')), may hold values from 0.25 to 1
- w_gate: bfloat16 [4, 7168, 2048], P('node', None, 'local'), may hold values from -0.0625 to 0.0625
- w_up: bfloat16 [4, 7168, 2048], P('node', None, 'local'), may hold values from -0.0625 to 0.0625
- w_down: bfloat16 [4, 2048, 7168], P('node', 'local'), may hold values from -0.125 to 0.125
Outputs:
- mixed_out: bfloat16 [2, 96, 7168], P(None, ('section', 'node', 'local'))
Inputs may be any that keep to these rules, and one draw needn't show every extreme that they name: `routes`: each row names 2 different experts. Among the 3 events of one device in one microbatch (an aligned block of rows), no expert is named more than 2 times, a bound that some block reaches.
All inputs are finite; a program needn't handle non-finite values.
Results may differ from a plain program's by a relative error of at most 0.011.
Values may be sent and summed in bfloat16 or wider, within the bound.
A program may use at most 64 MiB of HBM per device.

v0:
```python
import jax
import jax.numpy as jnp
from jax import lax
from jax.sharding import PartitionSpec as P


def shifted(value, axis, steps):
    count = lax.axis_size(axis)
    pairs = [(source, (source + steps) % count) for source in range(count)]
    return lax.ppermute(value, axis, pairs)


def route_through(dispatched, w_gate, w_up, w_down):
    micro_count, groups, capacity, model_width = dispatched.shape
    received = lax.all_to_all(dispatched, "node", split_axis=1, concat_axis=1, tiled=True)
    received_rows = received.reshape(micro_count * groups * capacity, model_width)
    gate_slice = w_gate[0]
    up_slice = w_up[0]
    down_slice = w_down[0]
    row_piece = lax.all_gather(received_rows, "local", axis=0, tiled=True)
    gate_act = jnp.dot(row_piece, gate_slice, preferred_element_type=jnp.float32)
    up_act = jnp.dot(row_piece, up_slice, preferred_element_type=jnp.float32)
    hidden = (jax.nn.silu(gate_act) * up_act).astype(jnp.bfloat16)
    summed = lax.psum_scatter(
        jnp.dot(hidden, down_slice, preferred_element_type=jnp.float32).astype(jnp.bfloat16),
        "local",
        scatter_dimension=0,
        tiled=True,
    )
    outgoing = summed.reshape(micro_count, groups, capacity, model_width)
    return lax.all_to_all(outgoing, "node", split_axis=1, concat_axis=1, tiled=True)


def shards(tokens, norm_gain, routes, gate_weight, w_gate, w_up, w_down):
    arrived = shifted(tokens, "section", 1)
    wide = arrived.astype(jnp.float32)
    mean_square = jnp.mean(wide * wide, axis=2, keepdims=True)
    normed = (wide * lax.rsqrt(mean_square + 1e-06) * norm_gain).astype(jnp.bfloat16)
    groups = lax.axis_size("node")
    tok_count = tokens.shape[1]
    capacity = min(tok_count, max(2, (tok_count * routes.shape[2] + groups - 1) // groups))
    chosen = routes[:, :, :, None] == jnp.arange(groups, dtype=jnp.int32)
    picked = jnp.sum(chosen.astype(jnp.int32), axis=2)
    weight = jnp.sum(jnp.where(chosen, gate_weight[:, :, :, None], 0.0), axis=2)
    slot_rank = jnp.cumsum(picked, axis=1) - 1
    placed = (picked[..., None] > 0) & (
        slot_rank[..., None] == jnp.arange(capacity, dtype=jnp.int32)
    )
    placement_matrix = placed.astype(jnp.bfloat16)
    dispatched = jnp.einsum(
        "mtec,mtd->mecd", placement_matrix, normed, preferred_element_type=jnp.float32
    ).astype(jnp.bfloat16)
    returned = jnp.concatenate(
        [
            route_through(dispatched[micro_index : micro_index + 1], w_gate, w_up, w_down)
            for micro_index in range(dispatched.shape[0])
        ],
        axis=0,
    )
    gathered = jnp.einsum(
        "mtec,mecd->mted", placement_matrix, returned, preferred_element_type=jnp.float32
    )
    mixed_out = wide + jnp.sum(weight[..., None] * gathered, axis=2)
    return mixed_out.astype(jnp.bfloat16)


def solution(mesh):
    placed = (
        P(None, ("section", "node", "local"), None),
        P(),
        P(None, ("section", "node", "local"), None),
        P(None, ("section", "node", "local"), None),
        P("node", None, "local"),
        P("node", None, "local"),
        P("node", "local", None),
    )
    return jax.shard_map(
        shards,
        mesh=mesh,
        in_specs=placed,
        out_specs=P(None, ("section", "node", "local"), None),
        check_vma=False,
    )
```

profile of v0, /device:TPU:0, one launch (start us, length us, event | category | flops | bytes accessed | tf_op | source)
XLA Modules:
  0.0 126.4 jit_solution(5805644876777825910)
XLA Ops:
  6.5 0.9 copy.29
  7.5 3.0 %collective-permute-start = (bf16[2,3,7168]{2,1,0:T(4,128)(2,1)S(1)}, bf16[2,3,7168]{2,1,0:T(4,128)(2,1)S(1)}, u32[]{:S(2)}, u32[]{:S(2)}) collective-permute-start(bf16[2,3,7168]{2,1,0:T(4,128)(2,1)S(1)} %copy.29), channel_id=1, source_target_pairs={{0,16},{16,0},{1,17},{17,1},{2,18},{18,2},{3,19},{19,3},{4,20},{20... | collective-permute-start | bytes 258056 | tf_op jit(solution)/shard_map/ppermute | solution.py:10
  10.5 0.8 copy.30
  11.3 0.1 convert_reduce_fusion
  11.4 0.1 copy.34
  11.5 0.1 copy.33
  11.7 2.0 %collective-permute-done = bf16[2,3,7168]{2,1,0:T(4,128)(2,1)S(1)} collective-permute-done((bf16[2,3,7168]{2,1,0:T(4,128)(2,1)S(1)}, bf16[2,3,7168]{2,1,0:T(4,128)(2,1)S(1)}, u32[]{:S(2)}, u32[]{:S(2)}) %collective-permute-start) | collective-permute-done | bytes 86048 | tf_op jit(solution)/shard_map/ppermute | solution.py:10
  13.6 0.2 fusion.28
  13.8 1.0 convolution_convert_fusion.2
  14.8 0.1 fusion.55
  14.9 0.7 copy.38
  15.7 3.3 %all-to-all-start.2 = ((bf16[1,4,2,7168]{3,2,0,1:T(2,128)(2,1)}), bf16[1,4,2,7168]{3,2,0,1:T(2,128)(2,1)S(1)}, u32[]{:S(2)}, u32[]{:S(2)}) async-start(bf16[1,4,2,7168]{3,2,0,1:T(2,128)(2,1)} %copy.38), calls=%async_computation.3 | async-start | bytes 229376 | tf_op jit(solution)/shard_map/all_to_all | solution.py:15
  19.0 0.7 copy.36
  19.7 3.7 %all-to-all-done.2 = bf16[1,4,2,7168]{3,2,0,1:T(2,128)(2,1)S(1)} async-done(((bf16[1,4,2,7168]{3,2,0,1:T(2,128)(2,1)}), bf16[1,4,2,7168]{3,2,0,1:T(2,128)(2,1)S(1)}, u32[]{:S(2)}, u32[]{:S(2)}) %all-to-all-start.2) | async-done | bytes 114720 | tf_op jit(solution)/shard_map/all_to_all | solution.py:15
  23.4 3.3 %all-to-all-start = ((bf16[1,4,2,7168]{3,2,0,1:T(2,128)(2,1)}), bf16[1,4,2,7168]{3,2,0,1:T(2,128)(2,1)S(1)}, u32[]{:S(2)}, u32[]{:S(2)}) async-start(bf16[1,4,2,7168]{3,2,0,1:T(2,128)(2,1)} %copy.36), calls=%async_computation | async-start | bytes 229376 | tf_op jit(solution)/shard_map/all_to_all | solution.py:15
  26.7 0.0 reduce-scatter.5.cloned.1.call-start
  26.8 15.9 %all_gather.7 = bf16[32,7168]{1,0:T(8,128)(2,1)S(1)} all-gather(bf16[8,7168]{1,0:T(8,128)(2,1)S(1)} %reshape.37), channel_id=1, replica_groups=mesh['section'=2,'node'=4,'local'=4] {'local'}, dimensions={0}, use_global_device_ids=true | all-gather | bytes 573440 | tf_op jit(solution)/shard_map/all_gather | solution.py:20
  42.8 4.4 %fusion.7 = f32[32,512]{1,0:T(8,128)S(1)} fusion(bf16[32,7168]{1,0:T(8,128)(2,1)S(1)} %all_gather.7, bf16[1,7168,512]{2,1,0:T(8,128)(2,1)} %param.11), kind=kOutput, calls=%fused_computation.11 | convolution fusion | flops 234881024 | bytes 7864320 | tf_op jit(solution)/shard_map/dot_general | solution.py:21
  47.2 8.7 %convolution_convert_fusion = bf16[32,7168]{1,0:T(8,128)(2,1)} fusion(bf16[1,512,7168]{2,1,0:T(8,128)(2,1)} %param.13, bf16[32,7168]{1,0:T(8,128)(2,1)S(1)} %all_gather.7, bf16[1,7168,512]{2,1,0:T(8,128)(2,1)} %param.12, f32[32,512]{1,0:T(8,128)S(1)} %fusion.7), kind=kOutput, calls=%fused_computation.2 | convolution fusion | flops 470089728 | bytes 15663104 | tf_op jit(solution)/shard_map/dot_general | solution.py:25
  55.8 0.0 reduce-scatter.5.cloned.1.call-update
  55.9 0.0 reduce-scatter.3.cloned.1.call-start
  55.9 0.0 all-to-all-done
  56.0 18.5 %all_gather.6 = bf16[32,7168]{1,0:T(8,128)(2,1)S(1)} all-gather(bf16[8,7168]{1,0:T(8,128)(2,1)S(1)} %reshape.35), channel_id=1, replica_groups=mesh['section'=2,'node'=4,'local'=4] {'local'}, dimensions={0}, use_global_device_ids=true | all-gather | bytes 573440 | tf_op jit(solution)/shard_map/all_gather | solution.py:20
  74.5 4.4 %fusion.9 = f32[32,512]{1,0:T(8,128)S(1)} fusion(bf16[32,7168]{1,0:T(8,128)(2,1)S(1)} %all_gather.6, bf16[1,7168,512]{2,1,0:T(8,128)(2,1)} %param.11), kind=kOutput, calls=%fused_computation.13 | convolution fusion | flops 234881024 | bytes 7864320 | tf_op jit(solution)/shard_map/dot_general | solution.py:21
  78.9 0.0 copy-start
  78.9 8.7 %convolution_convert_fusion.1 = bf16[32,7168]{1,0:T(8,128)(2,1)} fusion(bf16[1,512,7168]{2,1,0:T(8,128)(2,1)} %param.13, bf16[32,7168]{1,0:T(8,128)(2,1)S(1)} %all_gather.6, bf16[1,7168,512]{2,1,0:T(8,128)(2,1)} %param.12, f32[32,512]{1,0:T(8,128)S(1)} %fusion.9), kind=kOutput, calls=%fused_computation.3 | convolution fusion | flops 470089728 | bytes 15663104 | tf_op jit(solution)/shard_map/dot_general | solution.py:25
  87.6 0.0 reduce-scatter.3.cloned.1.call-update
  87.7 0.0 reduce-scatter.5.cloned.1.call-done
  87.7 1.6 %reshape.38 = bf16[1,4,2,7168]{3,2,1,0:T(2,128)(2,1)} reshape(bf16[8,7168]{1,0:T(8,128)(2,1)} %reduce-scatter.5.cloned.1.call-done) | data formatting | bytes 229376 | tf_op jit(solution)/shard_map/reshape | solution.py:30
  89.3 3.3 %all-to-all-start.3 = ((bf16[1,4,2,7168]{3,2,0,1:T(2,128)(2,1)}), bf16[1,4,2,7168]{3,2,0,1:T(2,128)(2,1)S(1)}, u32[]{:S(2)}, u32[]{:S(2)}) async-start(bf16[1,4,2,7168]{3,2,0,1:T(2,128)(2,1)} %bitcast.7), calls=%async_computation.5 | async-start | bytes 229376 | tf_op jit(solution)/shard_map/all_to_all | solution.py:31
  92.6 0.0 copy-done
  92.6 0.1 copy.31
  92.7 16.3 %reduce-scatter.3.cloned.1.call-done = bf16[8,7168]{1,0:T(8,128)(2,1)} async-done(((bf16[32,7168]{1,0:T(8,128)(2,1)}), bf16[8,7168]{1,0:T(8,128)(2,1)}) %reduce-scatter.3.cloned.1.call-update) | async-done | bytes 114704 | tf_op jit(solution)/shard_map/reduce_scatter | solution.py:24
  109.0 1.6 %reshape.36 = bf16[1,4,2,7168]{3,2,1,0:T(2,128)(2,1)} reshape(bf16[8,7168]{1,0:T(8,128)(2,1)} %reduce-scatter.3.cloned.1.call-done) | data formatting | bytes 229376 | tf_op jit(solution)/shard_map/reshape | solution.py:30
  110.6 0.0 all-to-all-done.3
  110.6 3.3 %all-to-all-start.1 = ((bf16[1,4,2,7168]{3,2,0,1:T(2,128)(2,1)}), bf16[1,4,2,7168]{3,2,0,1:T(2,128)(2,1)S(1)}, u32[]{:S(2)}, u32[]{:S(2)}) async-start(bf16[1,4,2,7168]{3,2,0,1:T(2,128)(2,1)} %bitcast.5), calls=%async_computation.2 | async-start | bytes 229376 | tf_op jit(solution)/shard_map/all_to_all | solution.py:31
  113.9 0.1 select_reduce_fusion
  114.0 0.1 copy.32
  114.1 4.2 %all-to-all-done.1 = bf16[1,4,2,7168]{3,2,0,1:T(2,128)(2,1)S(1)} async-done(((bf16[1,4,2,7168]{3,2,0,1:T(2,128)(2,1)}), bf16[1,4,2,7168]{3,2,0,1:T(2,128)(2,1)S(1)}, u32[]{:S(2)}, u32[]{:S(2)}) %all-to-all-start.1) | async-done | bytes 114720 | tf_op jit(solution)/shard_map/all_to_all | solution.py:31
  118.3 0.5 fusion.11
  118.8 0.1 fusion.31
  118.9 0.7 copy.42
  (7 shorter events, 0.2 us)
Async XLA Ops:
  7.5 6.2 %collective-permute-start = (bf16[2,3,7168]{2,1,0:T(4,128)(2,1)S(1)}, bf16[2,3,7168]{2,1,0:T(4,128)(2,1)S(1)}, u32[]{:S(2)}, u32[]{:S(2)}) collective-permute-start(bf16[2,3,7168]{2,1,0:T(4,128)(2,1)S(1)} %copy.29), channel_id=1, source_target_pairs={{0,16},{16,0},{1,17},{17,1},{2,18},{18,2},{3,19},{19,3},{4,20},{20... | collective-permute-start | bytes 258056 | tf_op jit(solution)/shard_map/ppermute | solution.py:10
  15.7 7.7 %all-to-all-start.2 = ((bf16[1,4,2,7168]{3,2,0,1:T(2,128)(2,1)}), bf16[1,4,2,7168]{3,2,0,1:T(2,128)(2,1)S(1)}, u32[]{:S(2)}, u32[]{:S(2)}) async-start(bf16[1,4,2,7168]{3,2,0,1:T(2,128)(2,1)} %copy.38), calls=%async_computation.3 | async-start | bytes 229376 | tf_op jit(solution)/shard_map/all_to_all | solution.py:15
  23.4 32.5 %all-to-all-start = ((bf16[1,4,2,7168]{3,2,0,1:T(2,128)(2,1)}), bf16[1,4,2,7168]{3,2,0,1:T(2,128)(2,1)S(1)}, u32[]{:S(2)}, u32[]{:S(2)}) async-start(bf16[1,4,2,7168]{3,2,0,1:T(2,128)(2,1)} %copy.36), calls=%async_computation | async-start | bytes 229376 | tf_op jit(solution)/shard_map/all_to_all | solution.py:15
  26.7 60.9 %reduce-scatter.5.cloned.1.call-start = ((), (), s32[]{:S(2)}) async-start(), calls=%async_computation.7 | async-start | bytes 573440 | tf_op jit(solution)/shard_map/reduce_scatter | solution.py:24
  55.9 53.1 %reduce-scatter.3.cloned.1.call-start = ((), (), s32[]{:S(2)}) async-start(), calls=%async_computation.6 | async-start | bytes 573440 | tf_op jit(solution)/shard_map/reduce_scatter | solution.py:24
  78.9 13.7 %copy-start = (f32[2,3,2]{1,2,0:T(2,128)S(1)}, f32[2,3,2]{1,2,0:T(2,128)}, u32[]{:S(2)}) copy-start(f32[2,3,2]{1,2,0:T(2,128)} %param.10) | copy-start | bytes 148
  89.3 21.3 %all-to-all-start.3 = ((bf16[1,4,2,7168]{3,2,0,1:T(2,128)(2,1)}), bf16[1,4,2,7168]{3,2,0,1:T(2,128)(2,1)S(1)}, u32[]{:S(2)}, u32[]{:S(2)}) async-start(bf16[1,4,2,7168]{3,2,0,1:T(2,128)(2,1)} %bitcast.7), calls=%async_computation.5 | async-start | bytes 229376 | tf_op jit(solution)/shard_map/all_to_all | solution.py:31
  110.6 7.7 %all-to-all-start.1 = ((bf16[1,4,2,7168]{3,2,0,1:T(2,128)(2,1)}), bf16[1,4,2,7168]{3,2,0,1:T(2,128)(2,1)S(1)}, u32[]{:S(2)}, u32[]{:S(2)}) async-start(bf16[1,4,2,7168]{3,2,0,1:T(2,128)(2,1)} %bitcast.5), calls=%async_computation.2 | async-start | bytes 229376 | tf_op jit(solution)/shard_map/all_to_all | solution.py:31
Sparse Core Ops, SparseCore 0:
  56.0 23.8 reduce-scatter.4
  87.8 21.1 reduce-scatter.2
where the time goes:
time: 127 us; the launch traced here: 126 us
  blocking collectives  34.4 us (27%)
  matrix products  27.7 us (22%)
  waiting for transfers between devices  26.2 us (21%)
  starting transfers between devices  16.4 us (13%)
  between operations  13.5 us (11%)
  local copies, waits for them, and re-layouts  7.64 us (6%)
    all_gather x2, blocking collectives, route_through(): row_piece = lax.all_gather(received_rows, 'local', axis=0, tiled=True)  34.4 us
    dot_general x2, matrix products, route_through(): jnp.dot(hidden, down_slice, preferred_element_type=jnp.float32)  17.4 us
    reduce_scatter x2, waiting for transfers between devices, route_through(): lax.psum_scatter(jnp.dot(hidden, down_slice, preferred_element_type=jnp.f...  16.3 us
    dot_general x2, matrix products, route_through(): jnp.dot(row_piece, gate_slice, preferred_element_type=jnp.float32)  8.85 us
    all_to_all x2, starting transfers between devices, route_through(): lax.all_to_all(outgoing, 'node', split_axis=1, concat_axis=1, tiled=True)  6.63 us
    all_to_all x2, starting transfers between devices, route_through(): lax.all_to_all(dispatched, 'node', split_axis=1, concat_axis=1, tiled=True)  6.63 us
    all_to_all x2, waiting for transfers between devices, route_through(): lax.all_to_all(outgoing, 'node', split_axis=1, concat_axis=1, tiled=True)  4.23 us
    all_to_all x2, waiting for transfers between devices, route_through(): lax.all_to_all(dispatched, 'node', split_axis=1, concat_axis=1, tiled=True)  3.69 us
  transfers between devices with their start and end apart: 7, of which 4 were waited for; matrix products, arithmetic and copies ran while one was open for 25% of the time, Pallas kernels for 0%

commit v1 on v0

v1 whole, which is shorter than its diff:
```python
import functools

import jax
import jax.numpy as jnp
from jax import lax
from jax.experimental import pallas as pl
from jax.experimental.pallas import tpu as pltpu
from jax.sharding import PartitionSpec as P

MESH = pl.DeviceIdType.MESH
BLOCK = 8
LANES = 128


def kernel(
    sections, locals_, chunks,
    tokens, gain, routes, gate_weight, w_gate, w_up, w_down,
    out,
    gate_v, up_v, down_v, wide_rows, normed, rows, gate_acc, up_acc, arrived,
    own_weights, all_weights, parts, core_in, pair_in, sums, local_in,
    load_sem, a_send, a_recv, w1_send, w1_recv, w2_send, w2_recv,
    s1_send, s1_recv, s2_send, s2_recv, r1_send, r1_recv, r2_send, r2_recv, r3_send, r3_recv,
):
    micro, tok, width = tokens.shape
    step = width // chunks
    total = rows.shape[0] * locals_ * BLOCK
    section, node, local = (lax.axis_index(name) for name in ("section", "node", "local"))
    ahead = lax.rem(section + 1, sections)
    behind = lax.rem(section + sections - 1, sections)
    near, far, cross = node ^ 1, node ^ 2, node ^ 3

    def cut(k):
        return pl.ds(pl.multiple_of(k * step, step), step)

    def peer(offset):
        return lax.rem(local + offset, locals_)

    def each(first, last, body):
        lax.fori_loop(first, last, lambda k, c: (body(k), c)[1], 0)

    def send(src, dst, send_sem, recv_sem, to):
        return pltpu.make_async_remote_copy(
            src_ref=src, dst_ref=dst, send_sem=send_sem, recv_sem=recv_sem,
            device_id=to, device_id_type=MESH,
        )

    def gate_load(k):
        return pltpu.make_async_copy(w_gate.at[0, cut(k), :], gate_v.at[cut(k), :], load_sem.at[0, k])

    def up_load(k):
        return pltpu.make_async_copy(w_up.at[0, cut(k), :], up_v.at[cut(k), :], load_sem.at[1, k])

    def down_load(k):
        return pltpu.make_async_copy(w_down.at[0, :, cut(k)], down_v.at[:, cut(k)], load_sem.at[2, k])

    def start_in(k):
        gate_load(k).start()
        up_load(k).start()

    each(0, chunks, start_in)
    each(0, chunks, lambda k: down_load(k).start())

    barrier = pltpu.get_barrier_semaphore()
    for other in range(locals_):
        pl.semaphore_signal(barrier, inc=1, device_id=(behind, node, other), device_id_type=MESH)
    for offset in range(1, locals_):
        pl.semaphore_signal(barrier, inc=1, device_id=(section, node, peer(offset)), device_id_type=MESH)
    for other in (near, far):
        pl.semaphore_signal(barrier, inc=1, device_id=(section, other, local), device_id_type=MESH)

    own_weights[...] = jnp.zeros_like(own_weights)
    lane = lax.broadcasted_iota(jnp.int32, (tok, LANES), 1)
    for m in range(micro):
        spread = jnp.zeros((tok, LANES), jnp.float32)
        for t in range(routes.shape[2]):
            spread += jnp.where(routes[m, :, t:t + 1] == lane, gate_weight[m, :, t:t + 1], 0.0)
        own_weights[m * tok:(m + 1) * tok, :] = spread

    wide_rows[...] = jnp.zeros_like(wide_rows)
    for m in range(micro):
        wide = tokens[m].astype(jnp.float32)
        mean_square = jnp.mean(wide * wide, axis=1, keepdims=True)
        wide_rows[m * tok:(m + 1) * tok, :] = wide * lax.rsqrt(mean_square + 1e-06) * gain[...]
    normed[...] = wide_rows[...].astype(jnp.bfloat16)

    pl.semaphore_wait(barrier, 2 * locals_ + 1)

    def w_out(offset):
        return send(own_weights, all_weights.at[node, local], w1_send.at[offset], w1_recv.at[local],
                    (section, node, peer(offset)))

    for offset in range(1, locals_):
        w_out(offset).start()
    all_weights[node, local] = own_weights[...]

    def s1(k, offset):
        return send(normed.at[:, cut(k)], rows.at[node, local, :, cut(k)],
                    s1_send.at[k, offset], s1_recv.at[k, local], (ahead, node, peer(offset)))

    def s1_wait(k):
        for other in range(locals_):
            send(normed.at[:, cut(k)], rows.at[node, other, :, cut(k)],
                 s1_send.at[k, other], s1_recv.at[k, other], (ahead, node, local)).wait_recv()

    def s1_start(k):
        for offset in range(locals_):
            s1(k, offset).start()

    each(0, chunks, s1_start)
    carry = send(tokens, arrived, a_send, a_recv, (ahead, node, local))
    carry.start()

    def s2(k, which, block, to):
        return send(rows.at[block, :, :, cut(k)], rows.at[block, :, :, cut(k)],
                    s2_send.at[k, which], s2_recv.at[k, which], (section, to, local))

    gate_acc[...] = jnp.zeros_like(gate_acc)
    up_acc[...] = jnp.zeros_like(up_acc)

    def in_step(i):
        @pl.when(i < chunks)
        def _():
            s1_wait(i)
            s2(i, 0, node, far).start()
            s2(i, 1, node, near).start()

        @pl.when((i >= 1) & (i < chunks + 1))
        def _():
            k = i - 1
            s2(k, 0, far, far).wait_recv()
            s2(k, 2, far, near).start()

        @pl.when(i >= 2)
        def _():
            k = i - 2
            s2(k, 1, near, near).wait_recv()
            s2(k, 2, cross, near).wait_recv()
            gate_load(k).wait()
            up_load(k).wait()
            piece = rows[:, :, :, cut(k)].astype(jnp.float32).reshape(total, step).astype(jnp.bfloat16)
            gate_acc[...] += jnp.dot(piece, gate_v[cut(k), :], preferred_element_type=jnp.float32)
            up_acc[...] += jnp.dot(piece, up_v[cut(k), :], preferred_element_type=jnp.float32)

    def w2(which, block, to):
        return send(all_weights.at[block], all_weights.at[block],
                    w2_send.at[which], w2_recv.at[which], (section, to, local))

    for other in range(1, locals_):
        source = peer(other)
        send(own_weights, all_weights.at[node, source], w1_send.at[other], w1_recv.at[source],
             (section, node, source)).wait_recv()
    w2(0, node, far).start()
    w2(1, node, near).start()

    each(0, chunks + 2, in_step)

    w2(0, far, far).wait_recv()
    w2(2, far, near).start()

    gate = gate_acc[...]
    hidden = (gate / (1.0 + jnp.exp(-gate)) * up_acc[...]).astype(jnp.bfloat16)

    w2(1, near, near).wait_recv()
    w2(2, cross, near).wait_recv()
    lanes = lax.broadcasted_iota(jnp.int32, (total, LANES), 1)
    weight = jnp.sum(
        jnp.where(lanes == node, all_weights[...].reshape(total, LANES), 0.0), axis=1, keepdims=True
    )
    carry.wait_recv()
    wide_rows[...] = jnp.zeros_like(wide_rows)
    for m in range(micro):
        wide_rows[m * tok:(m + 1) * tok, :] = arrived[m].astype(jnp.float32)

    def r1(k, which, block):
        return send(parts.at[block, :, :, cut(k)], core_in.at[which, :, :, cut(k)],
                    r1_send.at[k, which], r1_recv.at[k, which], (section, near, local))

    def r2(k):
        return send(parts.at[far, :, :, cut(k)], pair_in.at[:, :, cut(k)],
                    r2_send.at[k], r2_recv.at[k], (section, far, local))

    def r3(k, offset):
        return send(sums.at[peer(offset), :, cut(k)], local_in.at[local, :, cut(k)],
                    r3_send.at[k, offset], r3_recv.at[k, local], (section, node, peer(offset)))

    def out_step(j):
        @pl.when(j < chunks)
        def _():
            down_load(j).wait()
            part = jnp.dot(hidden, down_v[:, cut(j)], preferred_element_type=jnp.float32) * weight
            parts[:, :, :, cut(j)] = part.reshape(parts.shape[:3] + (step,)).astype(jnp.bfloat16)
            r1(j, 1, cross).start()
            r1(j, 0, near).start()

        @pl.when((j >= 1) & (j < chunks + 1))
        def _():
            k = j - 1
            r1(k, 1, cross).wait_recv()
            r1(k, 0, near).wait_recv()
            both = parts[far, :, :, cut(k)].astype(jnp.float32) + core_in[1, :, :, cut(k)].astype(jnp.float32)
            parts[far, :, :, cut(k)] = both.astype(jnp.bfloat16)
            r2(k).start()

        @pl.when((j >= 2) & (j < chunks + 2))
        def _():
            k = j - 2
            r2(k).wait_recv()
            full = (
                parts[node, :, :, cut(k)].astype(jnp.float32)
                + core_in[0, :, :, cut(k)].astype(jnp.float32)
                + pair_in[:, :, cut(k)].astype(jnp.float32)
            )
            sums[:, :, cut(k)] = full.astype(jnp.bfloat16)
            for offset in range(1, locals_):
                r3(k, offset).start()

        @pl.when(j >= 3)
        def _():
            k = j - 3
            mixed = wide_rows[:, cut(k)] + sums[local, :, cut(k)].astype(jnp.float32)
            for offset in range(1, locals_):
                source = peer(offset)
                send(sums.at[source, :, cut(k)], local_in.at[source, :, cut(k)],
                     r3_send.at[k, offset], r3_recv.at[k, source], (section, node, source)).wait_recv()
                mixed += local_in[source, :, cut(k)].astype(jnp.float32)
            wide_rows[:, cut(k)] = mixed

    each(0, chunks + 3, out_step)
    for m in range(micro):
        out[m] = wide_rows[m * tok:(m + 1) * tok, :].astype(jnp.bfloat16)

    def drain(k):
        for offset in range(locals_):
            s1(k, offset).wait_send()
        s2(k, 0, node, far).wait_send()
        s2(k, 1, node, near).wait_send()
        s2(k, 2, far, near).wait_send()
        r1(k, 0, near).wait_send()
        r1(k, 1, cross).wait_send()
        r2(k).wait_send()
        for offset in range(1, locals_):
            r3(k, offset).wait_send()

    each(0, chunks, drain)
    carry.wait_send()
    for offset in range(1, locals_):
        w_out(offset).wait_send()
    w2(0, node, far).wait_send()
    w2(1, node, near).wait_send()
    w2(2, far, near).wait_send()


def shards(sections, nodes, locals_, tokens, norm_gain, routes, gate_weight, w_gate, w_up, w_down):
    width, hid = w_gate.shape[1:]
    chunks = 7
    total = nodes * locals_ * BLOCK
    bf, f32 = jnp.bfloat16, jnp.float32
    vmem, dma = pltpu.VMEM, pltpu.SemaphoreType.DMA
    here = pl.BlockSpec(memory_space=pltpu.VMEM)
    away = pl.BlockSpec(memory_space=pl.ANY)
    return pl.pallas_call(
        functools.partial(kernel, sections, locals_, chunks),
        out_shape=jax.ShapeDtypeStruct(tokens.shape, bf),
        in_specs=[here] * 4 + [away] * 3,
        out_specs=here,
        scratch_shapes=[
            vmem((width, hid), bf), vmem((width, hid), bf), vmem((hid, width), bf),
            vmem((BLOCK, width), f32), vmem((BLOCK, width), bf),
            vmem((nodes, locals_, BLOCK, width), bf),
            vmem((total, hid), f32), vmem((total, hid), f32),
            vmem(tokens.shape, bf),
            vmem((BLOCK, LANES), f32), vmem((nodes, locals_, BLOCK, LANES), f32),
            vmem((nodes, locals_, BLOCK, width), bf),
            vmem((2, locals_, BLOCK, width), bf),
            vmem((locals_, BLOCK, width), bf),
            vmem((locals_, BLOCK, width), bf),
            vmem((locals_, BLOCK, width), bf),
            dma((3, chunks)), dma, dma,
            dma((locals_,)), dma((locals_,)), dma((3,)), dma((3,)),
            dma((chunks, locals_)), dma((chunks, locals_)), dma((chunks, 3)), dma((chunks, 3)),
            dma((chunks, 2)), dma((chunks, 2)), dma((chunks,)), dma((chunks,)),
            dma((chunks, locals_)), dma((chunks, locals_)),
        ],
        compiler_params=pltpu.CompilerParams(
            collective_id=0, has_side_effects=True, vmem_limit_bytes=60 * 1024 * 1024
        ),
        cost_estimate=pl.CostEstimate(
            flops=6 * total * width * hid, bytes_accessed=6 * width * hid, transcendentals=total * hid
        ),
        name="expert_relay",
    )(tokens, norm_gain.reshape(1, width), routes, gate_weight, w_gate, w_up, w_down)


def solution(mesh):
    events = P(None, ("section", "node", "local"), None)
    sizes = (mesh.shape["section"], mesh.shape["node"], mesh.shape["local"])
    return jax.shard_map(
        functools.partial(shards, *sizes),
        mesh=mesh,
        in_specs=(events, P(), events, events, P("node", None, "local"), P("node", None, "local"), P("node", "local", None)),
        out_specs=events,
        check_vma=False,
    )
```

time: 127 us -> 63.5 us (0.50)
  Pallas kernels: 0 us -> 57.4 us
  blocking collectives: 34.4 us -> 0 us
  matrix products: 27.7 us -> 0 us
  waiting for transfers between devices: 26.2 us -> 0 us
  starting transfers between devices: 16.4 us -> 0 us
  between operations: 13.5 us -> 0.01 us
  local copies, waits for them, and re-layouts: 7.64 us -> 5.89 us
    pallas_call x0 -> x1, Pallas kernels: none -> 57.4 us  [shards(): pl.pallas_call(functools.partial(kernel, sections, locals_, chunks), out_...]
    all_gather x2 -> x0, blocking collectives: 34.4 us -> none  [route_through(): row_piece = lax.all_gather(received_rows, 'local', axis=0, tiled=True)]
    dot_general x6 -> x0, matrix products: 27.7 us -> none  [the longest x2 17.4 us: route_through(): jnp.dot(hidden, down_slice, preferred_element_type=jnp.float32)]
    reduce_scatter x2 -> x0, waiting for transfers between devices: 16.3 us -> none  [route_through(): lax.psum_scatter(jnp.dot(hidden, down_slice, preferred_element_type=jnp.f...]
    all_to_all x4 -> x0, starting transfers between devices: 13.3 us -> none  [the longest x2 6.63 us: route_through(): lax.all_to_all(outgoing, 'node', split_axis=1, concat_axis=1, tiled=True)]
    all_to_all x4 -> x0, waiting for transfers between devices: 7.91 us -> none  [the longest x2 4.23 us: route_through(): lax.all_to_all(outgoing, 'node', split_axis=1, concat_axis=1, tiled=True)]
    reshape x4 -> x0, local copies, waits for them, and re-layouts: 3.26 us -> none  [the longest x2 3.16 us: route_through(): outgoing = summed.reshape(micro_count, groups, capacity, model_width)]
    ppermute x1 -> x0, starting transfers between devices: 3.03 us -> none  [shifted(): return lax.ppermute(value, axis, pairs)]
  transfers between devices with their start and end apart: 7 -> 0, of which waited for: 4 -> 0; matrix products, arithmetic and copies ran while one was open for 25% -> 0% of each run, Pallas kernels for 0% -> 0%
where the time goes in v1:
time: 63.5 us; the launch traced here: 63.3 us
  Pallas kernels  57.4 us (90%)
  local copies, waits for them, and re-layouts  5.89 us (9%)
    pallas_call x1, Pallas kernels, shards(): pl.pallas_call(functools.partial(kernel, sections, locals_, chunks), out_...  57.4 us
    unnamed x3, local copies, waits for them, and re-layouts  4.28 us
    pallas_call x1, local copies, waits for them, and re-layouts, shards(): pl.pallas_call(functools.partial(kernel, sections, locals_, chunks), out_...  1.61 us

profile of v1, /device:TPU:0, one launch (start us, length us, event | category | flops | bytes accessed | tf_op | source)
XLA Modules:
  0.0 63.3 jit_solution(13846985333085051696)
XLA Ops:
  0.0 1.4 %copy.9.routes = s32[2,3,2]{2,1,0:T(4,128)} copy(s32[2,3,2]{1,2,0:T(2,128)} %param.9) | data formatting | bytes 96 | tf_op args[2]
  1.4 1.4 %copy.10.gate_weight = f32[2,3,2]{2,1,0:T(4,128)} copy(f32[2,3,2]{1,2,0:T(2,128)} %param.10) | data formatting | bytes 96 | tf_op args[3]
  2.7 1.6 %copy.8.tokens = bf16[2,3,7168]{2,1,0:T(4,128)(2,1)} copy(bf16[2,3,7168]{2,0,1:T(2,128)(2,1)} %param.7) | data formatting | bytes 172032 | tf_op args[0]
  4.3 57.4 %expert_relay.1 = bf16[2,3,7168]{2,1,0:T(4,128)(2,1)} custom-call(bf16[2,3,7168]{2,1,0:T(4,128)(2,1)} %copy.8.tokens, f32[1,7168]{1,0:T(1,128)} %bitcast.1, s32[2,3,2]{2,1,0:T(4,128)} %copy.9.routes, f32[2,3,2]{2,1,0:T(4,128)} %copy.10.gate_weight, bf16[1,7168,512]{2,1,0:T(8,128)(2,1)} %w_gate.1, bf16[1,7168,512]{2,1,0:T(8,128)(2,1)} %w_up.1, ...), custom_call_target="tpu_custom_call" | custom-call | flops 2818572288 | bytes 22020096 | tf_op jit(solution)/shard_map/expert_relay/pallas_call | solution.py:261
  61.7 1.6 %copy.11 = bf16[2,3,7168]{2,0,1:T(2,128)(2,1)} copy(bf16[2,3,7168]{2,1,0:T(4,128)(2,1)} %expert_relay.1) | data formatting | bytes 172032 | tf_op jit(solution)/shard_map/expert_relay/pallas_call | solution.py:261

commit v2 on v1

--- a/solution.py
+++ b/solution.py
@@ -10,6 +10,8 @@
 MESH = pl.DeviceIdType.MESH
 BLOCK = 8
 LANES = 128
+FAR_LAG = 2
+PAIR_LAG = 3
 
 
 def kernel(
@@ -21,7 +23,7 @@
     load_sem, a_send, a_recv, w1_send, w1_recv, w2_send, w2_recv,
     s1_send, s1_recv, s2_send, s2_recv, r1_send, r1_recv, r2_send, r2_recv, r3_send, r3_recv,
 ):
-    micro, tok, width = tokens.shape
+    tok, micro, width = tokens.shape
     step = width // chunks
     total = rows.shape[0] * locals_ * BLOCK
     section, node, local = (lax.axis_index(name) for name in ("section", "node", "local"))
@@ -69,18 +71,17 @@
         pl.semaphore_signal(barrier, inc=1, device_id=(section, other, local), device_id_type=MESH)
 
     own_weights[...] = jnp.zeros_like(own_weights)
-    lane = lax.broadcasted_iota(jnp.int32, (tok, LANES), 1)
-    for m in range(micro):
-        spread = jnp.zeros((tok, LANES), jnp.float32)
-        for t in range(routes.shape[2]):
-            spread += jnp.where(routes[m, :, t:t + 1] == lane, gate_weight[m, :, t:t + 1], 0.0)
-        own_weights[m * tok:(m + 1) * tok, :] = spread
+    lane = lax.broadcasted_iota(jnp.int32, (routes.shape[1], LANES), 1)
+    for t in range(tok):
+        for m in range(micro):
+            spread = jnp.where(routes[m, :, t:t + 1] == lane, gate_weight[m, :, t:t + 1], 0.0)
+            own_weights[t * micro + m:t * micro + m + 1, :] = jnp.sum(spread, axis=0, keepdims=True)
 
     wide_rows[...] = jnp.zeros_like(wide_rows)
-    for m in range(micro):
-        wide = tokens[m].astype(jnp.float32)
+    for t in range(tok):
+        wide = tokens[t].astype(jnp.float32)
         mean_square = jnp.mean(wide * wide, axis=1, keepdims=True)
-        wide_rows[m * tok:(m + 1) * tok, :] = wide * lax.rsqrt(mean_square + 1e-06) * gain[...]
+        wide_rows[t * micro:(t + 1) * micro, :] = wide * lax.rsqrt(mean_square + 1e-06) * gain[...]
     normed[...] = wide_rows[...].astype(jnp.bfloat16)
 
     pl.semaphore_wait(barrier, 2 * locals_ + 1)
@@ -124,15 +125,15 @@
             s2(i, 0, node, far).start()
             s2(i, 1, node, near).start()
 
-        @pl.when((i >= 1) & (i < chunks + 1))
-        def _():
-            k = i - 1
+        @pl.when((i >= FAR_LAG) & (i < chunks + FAR_LAG))
+        def _():
+            k = i - FAR_LAG
             s2(k, 0, far, far).wait_recv()
             s2(k, 2, far, near).start()
 
-        @pl.when(i >= 2)
-        def _():
-            k = i - 2
+        @pl.when(i > FAR_LAG)
+        def _():
+            k = i - FAR_LAG - 1
             s2(k, 1, near, near).wait_recv()
             s2(k, 2, cross, near).wait_recv()
             gate_load(k).wait()
@@ -152,7 +153,7 @@
     w2(0, node, far).start()
     w2(1, node, near).start()
 
-    each(0, chunks + 2, in_step)
+    each(0, chunks + FAR_LAG + 1, in_step)
 
     w2(0, far, far).wait_recv()
     w2(2, far, near).start()
@@ -168,8 +169,8 @@
     )
     carry.wait_recv()
     wide_rows[...] = jnp.zeros_like(wide_rows)
-    for m in range(micro):
-        wide_rows[m * tok:(m + 1) * tok, :] = arrived[m].astype(jnp.float32)
+    for t in range(tok):
+        wide_rows[t * micro:(t + 1) * micro, :] = arrived[t].astype(jnp.float32)
 
     def r1(k, which, block):
         return send(parts.at[block, :, :, cut(k)], core_in.at[which, :, :, cut(k)],
@@ -201,9 +202,9 @@
             parts[far, :, :, cut(k)] = both.astype(jnp.bfloat16)
             r2(k).start()
 
-        @pl.when((j >= 2) & (j < chunks + 2))
-        def _():
-            k = j - 2
+        @pl.when(j >= PAIR_LAG)
+        def _():
+            k = j - PAIR_LAG
             r2(k).wait_recv()
             full = (
                 parts[node, :, :, cut(k)].astype(jnp.float32)
@@ -214,20 +215,19 @@
             for offset in range(1, locals_):
                 r3(k, offset).start()
 
-        @pl.when(j >= 3)
-        def _():
-            k = j - 3
-            mixed = wide_rows[:, cut(k)] + sums[local, :, cut(k)].astype(jnp.float32)
-            for offset in range(1, locals_):
-                source = peer(offset)
-                send(sums.at[source, :, cut(k)], local_in.at[source, :, cut(k)],
-                     r3_send.at[k, offset], r3_recv.at[k, source], (section, node, source)).wait_recv()
-                mixed += local_in[source, :, cut(k)].astype(jnp.float32)
-            wide_rows[:, cut(k)] = mixed
-
-    each(0, chunks + 3, out_step)
-    for m in range(micro):
-        out[m] = wide_rows[m * tok:(m + 1) * tok, :].astype(jnp.bfloat16)
+    def last_step(k):
+        mixed = wide_rows[:, cut(k)] + sums[local, :, cut(k)].astype(jnp.float32)
+        for offset in range(1, locals_):
+            source = peer(offset)
+            send(sums.at[source, :, cut(k)], local_in.at[source, :, cut(k)],
+                 r3_send.at[k, offset], r3_recv.at[k, source], (section, node, source)).wait_recv()
+            mixed += local_in[source, :, cut(k)].astype(jnp.float32)
+        wide_rows[:, cut(k)] = mixed
+
+    each(0, chunks + PAIR_LAG, out_step)
+    each(0, chunks, last_step)
+    for t in range(tok):
+        out[t] = wide_rows[t * micro:(t + 1) * micro, :].astype(jnp.bfloat16)
 
     def drain(k):
         for offset in range(locals_):
@@ -258,7 +258,8 @@
     vmem, dma = pltpu.VMEM, pltpu.SemaphoreType.DMA
     here = pl.BlockSpec(memory_space=pltpu.VMEM)
     away = pl.BlockSpec(memory_space=pl.ANY)
-    return pl.pallas_call(
+    tokens = tokens.transpose(1, 0, 2)
+    mixed = pl.pallas_call(
         functools.partial(kernel, sections, locals_, chunks),
         out_shape=jax.ShapeDtypeStruct(tokens.shape, bf),
         in_specs=[here] * 4 + [away] * 3,
@@ -288,7 +289,11 @@
             flops=6 * total * width * hid, bytes_accessed=6 * width * hid, transcendentals=total * hid
         ),
         name="expert_relay",
-    )(tokens, norm_gain.reshape(1, width), routes, gate_weight, w_gate, w_up, w_down)
+    )(
+        tokens, norm_gain.reshape(1, width), routes.transpose(0, 2, 1), gate_weight.transpose(0, 2, 1),
+        w_gate, w_up, w_down,
+    )
+    return mixed.transpose(1, 0, 2)
 
 
 def solution(mesh):

time: 63.5 us -> 49.9 us (0.79)
  Pallas kernels: 57.4 us -> 48.1 us
  local copies, waits for them, and re-layouts: 5.89 us -> 1.59 us
    pallas_call x1, Pallas kernels: 57.4 us -> 48.1 us  [shards(): pl.pallas_call(functools.partial(kernel, sections, locals_, chunks), out_...]
    unnamed x3 -> x1, local copies, waits for them, and re-layouts: 4.28 us -> 1.59 us
    pallas_call x1 -> x0, local copies, waits for them, and re-layouts: 1.61 us -> none  [shards(): pl.pallas_call(functools.partial(kernel, sections, locals_, chunks), out_...]
where the time goes in v2:
time: 49.9 us; the launch traced here: 49.7 us
  Pallas kernels  48.1 us (96%)
  local copies, waits for them, and re-layouts  1.59 us (3%)
    pallas_call x1, Pallas kernels, shards(): pl.pallas_call(functools.partial(kernel, sections, locals_, chunks), out_...  48.1 us
    unnamed x1, local copies, waits for them, and re-layouts  1.59 us

profile of v2, /device:TPU:0, one launch (start us, length us, event | category | flops | bytes accessed | tf_op | source)
XLA Modules:
  0.0 49.7 jit_solution(11035681183259261031)
XLA Ops:
  0.0 48.1 %expert_relay.1 = bf16[3,2,7168]{2,1,0:T(2,128)(2,1)} custom-call(bf16[3,2,7168]{2,1,0:T(2,128)(2,1)} %bitcast.6, f32[1,7168]{1,0:T(1,128)} %bitcast.7, s32[2,2,3]{2,1,0:T(2,128)} %bitcast.8, f32[2,2,3]{2,1,0:T(2,128)} %bitcast.9, bf16[1,7168,512]{2,1,0:T(8,128)(2,1)} %w_gate.1, bf16[1,7168,512]{2,1,0:T(8,128)(2,1)} %w_up.1, bf16[1,512,7168]{2,1,0:T(8,128)(2,1)} %w_down.1), custom_call_target="tpu_custom_call" | custom-call | flops 2818572288 | bytes 22020096 | tf_op jit(solution)/shard_map/expert_relay/pallas_call | solution.py:262
  48.1 1.6 %copy.9 = bf16[2,3,7168]{2,0,1:T(2,128)(2,1)} copy(bf16[2,3,7168]{2,0,1:T(2,128)(2,1)} %bitcast.5) | data formatting | bytes 172032

commit v3 on v2

--- a/solution.py
+++ b/solution.py
@@ -12,20 +12,25 @@
 LANES = 128
 FAR_LAG = 2
 PAIR_LAG = 3
+PIECES = 4
 
 
 def kernel(
     sections, locals_, chunks,
     tokens, gain, routes, gate_weight, w_gate, w_up, w_down,
     out,
-    gate_v, up_v, down_v, wide_rows, normed, rows, gate_acc, up_acc, arrived,
-    own_weights, all_weights, parts, core_in, pair_in, sums, local_in,
+    gate_v, up_v, down_v, wide_rows, packed, rows_in, rows, gate_acc, up_acc, arrived,
+    own_weights, all_weights, row_weights, packing, spreading, parts, core_in, pair_in, sums, local_in,
     load_sem, a_send, a_recv, w1_send, w1_recv, w2_send, w2_recv,
     s1_send, s1_recv, s2_send, s2_recv, r1_send, r1_recv, r2_send, r2_recv, r3_send, r3_recv,
 ):
     tok, micro, width = tokens.shape
     step = width // chunks
-    total = rows.shape[0] * locals_ * BLOCK
+    count = tok * micro
+    group = locals_ * count
+    total = rows.shape[0] * group
+    part = step // PIECES
+    pack = PIECES * count
     section, node, local = (lax.axis_index(name) for name in ("section", "node", "local"))
     ahead = lax.rem(section + 1, sections)
     behind = lax.rem(section + sections - 1, sections)
@@ -33,6 +38,9 @@
 
     def cut(k):
         return pl.ds(pl.multiple_of(k * step, step), step)
+
+    def narrow(k, p):
+        return pl.ds(pl.multiple_of(k * step + p * part, part), part)
 
     def peer(offset):
         return lax.rem(local + offset, locals_)
@@ -82,7 +90,15 @@
         wide = tokens[t].astype(jnp.float32)
         mean_square = jnp.mean(wide * wide, axis=1, keepdims=True)
         wide_rows[t * micro:(t + 1) * micro, :] = wide * lax.rsqrt(mean_square + 1e-06) * gain[...]
-    normed[...] = wide_rows[...].astype(jnp.bfloat16)
+    packing[...] = jnp.zeros_like(packing)
+    spreading[...] = jnp.zeros_like(spreading)
+
+    def pack_own(k):
+        for p in range(PIECES):
+            packing[0, p * count:p * count + BLOCK, :] = wide_rows[:, narrow(k, p)]
+        packed[k] = packing[0, 0:pack, :].astype(jnp.bfloat16)
+
+    each(0, chunks, pack_own)
 
     pl.semaphore_wait(barrier, 2 * locals_ + 1)
 
@@ -95,12 +111,12 @@
     all_weights[node, local] = own_weights[...]
 
     def s1(k, offset):
-        return send(normed.at[:, cut(k)], rows.at[node, local, :, cut(k)],
+        return send(packed.at[k], rows_in.at[k, local],
                     s1_send.at[k, offset], s1_recv.at[k, local], (ahead, node, peer(offset)))
 
     def s1_wait(k):
         for other in range(locals_):
-            send(normed.at[:, cut(k)], rows.at[node, other, :, cut(k)],
+            send(packed.at[k], rows_in.at[k, other],
                  s1_send.at[k, other], s1_recv.at[k, other], (ahead, node, local)).wait_recv()
 
     def s1_start(k):
@@ -112,7 +128,7 @@
     carry.start()
 
     def s2(k, which, block, to):
-        return send(rows.at[block, :, :, cut(k)], rows.at[block, :, :, cut(k)],
+        return send(rows.at[block, :, cut(k)], rows.at[block, :, cut(k)],
                     s2_send.at[k, which], s2_recv.at[k, which], (section, to, local))
 
     gate_acc[...] = jnp.zeros_like(gate_acc)
@@ -122,6 +138,13 @@
         @pl.when(i < chunks)
         def _():
             s1_wait(i)
+            for other in range(locals_):
+                packing[other, 0:pack, :] = rows_in[i, other].astype(jnp.float32)
+                for p in range(PIECES):
+                    spreading[other * count:other * count + BLOCK, p * part:(p + 1) * part] = (
+                        packing[other, p * count:p * count + BLOCK, :]
+                    )
+            rows[node, :, cut(i)] = spreading[0:group, :].astype(jnp.bfloat16)
             s2(i, 0, node, far).start()
             s2(i, 1, node, near).start()
 
@@ -138,7 +161,7 @@
             s2(k, 2, cross, near).wait_recv()
             gate_load(k).wait()
             up_load(k).wait()
-            piece = rows[:, :, :, cut(k)].astype(jnp.float32).reshape(total, step).astype(jnp.bfloat16)
+            piece = rows[:, :, cut(k)].astype(jnp.float32).reshape(total, step).astype(jnp.bfloat16)
             gate_acc[...] += jnp.dot(piece, gate_v[cut(k), :], preferred_element_type=jnp.float32)
             up_acc[...] += jnp.dot(piece, up_v[cut(k), :], preferred_element_type=jnp.float32)
 
@@ -163,33 +186,35 @@
 
     w2(1, near, near).wait_recv()
     w2(2, cross, near).wait_recv()
+    for block in range(rows.shape[0]):
+        for other in range(locals_):
+            first = block * group + other * count
+            row_weights[first:first + BLOCK, :] = all_weights[block, other]
     lanes = lax.broadcasted_iota(jnp.int32, (total, LANES), 1)
-    weight = jnp.sum(
-        jnp.where(lanes == node, all_weights[...].reshape(total, LANES), 0.0), axis=1, keepdims=True
-    )
+    weight = jnp.sum(jnp.where(lanes == node, row_weights[0:total, :], 0.0), axis=1, keepdims=True)
     carry.wait_recv()
     wide_rows[...] = jnp.zeros_like(wide_rows)
     for t in range(tok):
         wide_rows[t * micro:(t + 1) * micro, :] = arrived[t].astype(jnp.float32)
 
     def r1(k, which, block):
-        return send(parts.at[block, :, :, cut(k)], core_in.at[which, :, :, cut(k)],
+        return send(parts.at[block, :, cut(k)], core_in.at[which, :, cut(k)],
                     r1_send.at[k, which], r1_recv.at[k, which], (section, near, local))
 
     def r2(k):
-        return send(parts.at[far, :, :, cut(k)], pair_in.at[:, :, cut(k)],
+        return send(parts.at[far, :, cut(k)], pair_in.at[:, cut(k)],
                     r2_send.at[k], r2_recv.at[k], (section, far, local))
 
     def r3(k, offset):
-        return send(sums.at[peer(offset), :, cut(k)], local_in.at[local, :, cut(k)],
+        return send(sums.at[k, peer(offset)], local_in.at[k, local],
                     r3_send.at[k, offset], r3_recv.at[k, local], (section, node, peer(offset)))
 
     def out_step(j):
         @pl.when(j < chunks)
         def _():
             down_load(j).wait()
-            part = jnp.dot(hidden, down_v[:, cut(j)], preferred_element_type=jnp.float32) * weight
-            parts[:, :, :, cut(j)] = part.reshape(parts.shape[:3] + (step,)).astype(jnp.bfloat16)
+            term = jnp.dot(hidden, down_v[:, cut(j)], preferred_element_type=jnp.float32) * weight
+            parts[:, :, cut(j)] = term.reshape(parts.shape[:2] + (step,)).astype(jnp.bfloat16)
             r1(j, 1, cross).start()
             r1(j, 0, near).start()
 
@@ -198,31 +223,38 @@
             k = j - 1
             r1(k, 1, cross).wait_recv()
             r1(k, 0, near).wait_recv()
-            both = parts[far, :, :, cut(k)].astype(jnp.float32) + core_in[1, :, :, cut(k)].astype(jnp.float32)
-            parts[far, :, :, cut(k)] = both.astype(jnp.bfloat16)
+            both = parts[far, :, cut(k)].astype(jnp.float32) + core_in[1, :, cut(k)].astype(jnp.float32)
+            parts[far, :, cut(k)] = both.astype(jnp.bfloat16)
             r2(k).start()
 
         @pl.when(j >= PAIR_LAG)
         def _():
             k = j - PAIR_LAG
             r2(k).wait_recv()
-            full = (
-                parts[node, :, :, cut(k)].astype(jnp.float32)
-                + core_in[0, :, :, cut(k)].astype(jnp.float32)
-                + pair_in[:, :, cut(k)].astype(jnp.float32)
+            spreading[0:group, :] = (
+                parts[node, :, cut(k)].astype(jnp.float32)
+                + core_in[0, :, cut(k)].astype(jnp.float32)
+                + pair_in[:, cut(k)].astype(jnp.float32)
             )
-            sums[:, :, cut(k)] = full.astype(jnp.bfloat16)
+            for other in range(locals_):
+                for p in range(PIECES):
+                    packing[other, p * count:p * count + BLOCK, :] = (
+                        spreading[other * count:other * count + BLOCK, p * part:(p + 1) * part]
+                    )
+                sums[k, other] = packing[other, 0:pack, :].astype(jnp.bfloat16)
             for offset in range(1, locals_):
                 r3(k, offset).start()
 
     def last_step(k):
-        mixed = wide_rows[:, cut(k)] + sums[local, :, cut(k)].astype(jnp.float32)
+        mixed = sums[k, local].astype(jnp.float32)
         for offset in range(1, locals_):
             source = peer(offset)
-            send(sums.at[source, :, cut(k)], local_in.at[source, :, cut(k)],
+            send(sums.at[k, source], local_in.at[k, source],
                  r3_send.at[k, offset], r3_recv.at[k, source], (section, node, source)).wait_recv()
-            mixed += local_in[source, :, cut(k)].astype(jnp.float32)
-        wide_rows[:, cut(k)] = mixed
+            mixed += local_in[k, source].astype(jnp.float32)
+        packing[0, 0:pack, :] = mixed
+        for p in range(PIECES):
+            wide_rows[:, narrow(k, p)] += packing[0, p * count:p * count + BLOCK, :]
 
     each(0, chunks + PAIR_LAG, out_step)
     each(0, chunks, last_step)
@@ -253,7 +285,11 @@
 def shards(sections, nodes, locals_, tokens, norm_gain, routes, gate_weight, w_gate, w_up, w_down):
     width, hid = w_gate.shape[1:]
     chunks = 7
-    total = nodes * locals_ * BLOCK
+    count = tokens.shape[0] * tokens.shape[1]
+    group = locals_ * count
+    total = nodes * group
+    step = width // chunks
+    pack, part = PIECES * count, step // PIECES
     bf, f32 = jnp.bfloat16, jnp.float32
     vmem, dma = pltpu.VMEM, pltpu.SemaphoreType.DMA
     here = pl.BlockSpec(memory_space=pltpu.VMEM)
@@ -266,16 +302,19 @@
         out_specs=here,
         scratch_shapes=[
             vmem((width, hid), bf), vmem((width, hid), bf), vmem((hid, width), bf),
-            vmem((BLOCK, width), f32), vmem((BLOCK, width), bf),
-            vmem((nodes, locals_, BLOCK, width), bf),
+            vmem((BLOCK, width), f32), vmem((chunks, pack, part), bf),
+            vmem((chunks, locals_, pack, part), bf),
+            vmem((nodes, group, width), bf),
             vmem((total, hid), f32), vmem((total, hid), f32),
             vmem(tokens.shape, bf),
             vmem((BLOCK, LANES), f32), vmem((nodes, locals_, BLOCK, LANES), f32),
-            vmem((nodes, locals_, BLOCK, width), bf),
-            vmem((2, locals_, BLOCK, width), bf),
-            vmem((locals_, BLOCK, width), bf),
-            vmem((locals_, BLOCK, width), bf),
-            vmem((locals_, BLOCK, width), bf),
+            vmem((total + BLOCK, LANES), f32),
+            vmem((locals_, pack + BLOCK, part), f32), vmem((group + BLOCK, step), f32),
+            vmem((nodes, group, width), bf),
+            vmem((2, group, width), bf),
+            vmem((group, width), bf),
+            vmem((chunks, locals_, pack, part), bf),
+            vmem((chunks, locals_, pack, part), bf),
             dma((3, chunks)), dma, dma,
             dma((locals_,)), dma((locals_,)), dma((3,)), dma((3,)),
             dma((chunks, locals_)), dma((chunks, locals_)), dma((chunks, 3)), dma((chunks, 3)),

time: 49.9 us -> 45.5 us (0.912)
  Pallas kernels: 48.1 us -> 43.7 us
    pallas_call x1, Pallas kernels: 48.1 us -> 43.7 us  [shards(): pl.pallas_call(functools.partial(kernel, sections, locals_, chunks), out_...]
where the time goes in v3:
time: 45.5 us; the launch traced here: 45.3 us
  Pallas kernels  43.7 us (96%)
  local copies, waits for them, and re-layouts  1.59 us (3%)
    pallas_call x1, Pallas kernels, shards(): pl.pallas_call(functools.partial(kernel, sections, locals_, chunks), out_...  43.7 us
    unnamed x1, local copies, waits for them, and re-layouts  1.59 us

profile of v3, /device:TPU:0, one launch (start us, length us, event | category | flops | bytes accessed | tf_op | source)
XLA Modules:
  0.0 45.3 jit_solution(7762969449402833070)
XLA Ops:
  0.0 43.7 %expert_relay.1 = bf16[3,2,7168]{2,1,0:T(2,128)(2,1)} custom-call(bf16[3,2,7168]{2,1,0:T(2,128)(2,1)} %bitcast.6, f32[1,7168]{1,0:T(1,128)} %bitcast.7, s32[2,2,3]{2,1,0:T(2,128)} %bitcast.8, f32[2,2,3]{2,1,0:T(2,128)} %bitcast.9, bf16[1,7168,512]{2,1,0:T(8,128)(2,1)} %w_gate.1, bf16[1,7168,512]{2,1,0:T(8,128)(2,1)} %w_up.1, bf16[1,512,7168]{2,1,0:T(8,128)(2,1)} %w_down.1), custom_call_target="tpu_custom_call" | custom-call | flops 2113929216 | bytes 22020096 | tf_op jit(solution)/shard_map/expert_relay/pallas_call | solution.py:298
  43.7 1.6 %copy.9 = bf16[2,3,7168]{2,0,1:T(2,128)(2,1)} copy(bf16[2,3,7168]{2,0,1:T(2,128)(2,1)} %bitcast.5) | data formatting | bytes 172032

commit v4 on v3

--- a/solution.py
+++ b/solution.py
@@ -11,7 +11,8 @@
 BLOCK = 8
 LANES = 128
 FAR_LAG = 2
-PAIR_LAG = 3
+CORE_LAG = 2
+PAIR_LAG = 4
 PIECES = 4
 
 
@@ -67,9 +68,6 @@
         gate_load(k).start()
         up_load(k).start()
 
-    each(0, chunks, start_in)
-    each(0, chunks, lambda k: down_load(k).start())
-
     barrier = pltpu.get_barrier_semaphore()
     for other in range(locals_):
         pl.semaphore_signal(barrier, inc=1, device_id=(behind, node, other), device_id_type=MESH)
@@ -78,6 +76,9 @@
     for other in (near, far):
         pl.semaphore_signal(barrier, inc=1, device_id=(section, other, local), device_id_type=MESH)
 
+    each(0, chunks, start_in)
+    each(0, chunks, lambda k: down_load(k).start())
+
     own_weights[...] = jnp.zeros_like(own_weights)
     lane = lax.broadcasted_iota(jnp.int32, (routes.shape[1], LANES), 1)
     for t in range(tok):
@@ -133,6 +134,10 @@
 
     gate_acc[...] = jnp.zeros_like(gate_acc)
     up_acc[...] = jnp.zeros_like(up_acc)
+
+    def w2(which, block, to):
+        return send(all_weights.at[block], all_weights.at[block],
+                    w2_send.at[which], w2_recv.at[which], (section, to, local))
 
     def in_step(i):
         @pl.when(i < chunks)
@@ -148,6 +153,20 @@
             s2(i, 0, node, far).start()
             s2(i, 1, node, near).start()
 
+        @pl.when(i == 1)
+        def _():
+            for other in range(1, locals_):
+                source = peer(other)
+                send(own_weights, all_weights.at[node, source], w1_send.at[other], w1_recv.at[source],
+                     (section, node, source)).wait_recv()
+            w2(0, node, far).start()
+            w2(1, node, near).start()
+
+        @pl.when(i == chunks)
+        def _():
+            w2(0, far, far).wait_recv()
+            w2(2, far, near).start()
+
         @pl.when((i >= FAR_LAG) & (i < chunks + FAR_LAG))
         def _():
             k = i - FAR_LAG
@@ -165,21 +184,7 @@
             gate_acc[...] += jnp.dot(piece, gate_v[cut(k), :], preferred_element_type=jnp.float32)
             up_acc[...] += jnp.dot(piece, up_v[cut(k), :], preferred_element_type=jnp.float32)
 
-    def w2(which, block, to):
-        return send(all_weights.at[block], all_weights.at[block],
-                    w2_send.at[which], w2_recv.at[which], (section, to, local))
-
-    for other in range(1, locals_):
-        source = peer(other)
-        send(own_weights, all_weights.at[node, source], w1_send.at[other], w1_recv.at[source],
-             (section, node, source)).wait_recv()
-    w2(0, node, far).start()
-    w2(1, node, near).start()
-
     each(0, chunks + FAR_LAG + 1, in_step)
-
-    w2(0, far, far).wait_recv()
-    w2(2, far, near).start()
 
     gate = gate_acc[...]
     hidden = (gate / (1.0 + jnp.exp(-gate)) * up_acc[...]).astype(jnp.bfloat16)
@@ -192,10 +197,6 @@
             row_weights[first:first + BLOCK, :] = all_weights[block, other]
     lanes = lax.broadcasted_iota(jnp.int32, (total, LANES), 1)
     weight = jnp.sum(jnp.where(lanes == node, row_weights[0:total, :], 0.0), axis=1, keepdims=True)
-    carry.wait_recv()
-    wide_rows[...] = jnp.zeros_like(wide_rows)
-    for t in range(tok):
-        wide_rows[t * micro:(t + 1) * micro, :] = arrived[t].astype(jnp.float32)
 
     def r1(k, which, block):
         return send(parts.at[block, :, cut(k)], core_in.at[which, :, cut(k)],
@@ -210,6 +211,13 @@
                     r3_send.at[k, offset], r3_recv.at[k, local], (section, node, peer(offset)))
 
     def out_step(j):
+        @pl.when(j == chunks)
+        def _():
+            carry.wait_recv()
+            wide_rows[...] = jnp.zeros_like(wide_rows)
+            for t in range(tok):
+                wide_rows[t * micro:(t + 1) * micro, :] = arrived[t].astype(jnp.float32)
+
         @pl.when(j < chunks)
         def _():
             down_load(j).wait()
@@ -217,10 +225,15 @@
             parts[:, :, cut(j)] = term.reshape(parts.shape[:2] + (step,)).astype(jnp.bfloat16)
             r1(j, 1, cross).start()
             r1(j, 0, near).start()
-
-        @pl.when((j >= 1) & (j < chunks + 1))
-        def _():
-            k = j - 1
+            for offset in range(locals_):
+                s1(j, offset).wait_send()
+            s2(j, 0, node, far).wait_send()
+            s2(j, 1, node, near).wait_send()
+            s2(j, 2, far, near).wait_send()
+
+        @pl.when((j >= CORE_LAG) & (j < chunks + CORE_LAG))
+        def _():
+            k = j - CORE_LAG
             r1(k, 1, cross).wait_recv()
             r1(k, 0, near).wait_recv()
             both = parts[far, :, cut(k)].astype(jnp.float32) + core_in[1, :, cut(k)].astype(jnp.float32)
@@ -246,6 +259,11 @@
                 r3(k, offset).start()
 
     def last_step(k):
+        r1(k, 0, near).wait_send()
+        r1(k, 1, cross).wait_send()
+        r2(k).wait_send()
+        for offset in range(1, locals_):
+            r3(k, offset).wait_send()
         mixed = sums[k, local].astype(jnp.float32)
         for offset in range(1, locals_):
             source = peer(offset)
@@ -257,29 +275,16 @@
             wide_rows[:, narrow(k, p)] += packing[0, p * count:p * count + BLOCK, :]
 
     each(0, chunks + PAIR_LAG, out_step)
-    each(0, chunks, last_step)
-    for t in range(tok):
-        out[t] = wide_rows[t * micro:(t + 1) * micro, :].astype(jnp.bfloat16)
-
-    def drain(k):
-        for offset in range(locals_):
-            s1(k, offset).wait_send()
-        s2(k, 0, node, far).wait_send()
-        s2(k, 1, node, near).wait_send()
-        s2(k, 2, far, near).wait_send()
-        r1(k, 0, near).wait_send()
-        r1(k, 1, cross).wait_send()
-        r2(k).wait_send()
-        for offset in range(1, locals_):
-            r3(k, offset).wait_send()
-
-    each(0, chunks, drain)
     carry.wait_send()
     for offset in range(1, locals_):
         w_out(offset).wait_send()
     w2(0, node, far).wait_send()
     w2(1, node, near).wait_send()
     w2(2, far, near).wait_send()
+
+    each(0, chunks, last_step)
+    for t in range(tok):
+        out[t] = wide_rows[t * micro:(t + 1) * micro, :].astype(jnp.bfloat16)
 
 
 def shards(sections, nodes, locals_, tokens, norm_gain, routes, gate_weight, w_gate, w_up, w_down):

time: 45.5 us -> 44.4 us (0.976)
  Pallas kernels: 43.7 us -> 42.6 us
    pallas_call x1, Pallas kernels: 43.7 us -> 42.6 us  [shards(): pl.pallas_call(functools.partial(kernel, sections, locals_, chunks), out_...]
where the time goes in v4:
time: 44.4 us; the launch traced here: 44.2 us
  Pallas kernels  42.6 us (96%)
  local copies, waits for them, and re-layouts  1.59 us (4%)
    pallas_call x1, Pallas kernels, shards(): pl.pallas_call(functools.partial(kernel, sections, locals_, chunks), out_...  42.6 us
    unnamed x1, local copies, waits for them, and re-layouts  1.59 us

profile of v4, /device:TPU:0, one launch (start us, length us, event | category | flops | bytes accessed | tf_op | source)
XLA Modules:
  0.0 44.2 jit_solution(3803853109369077331)
XLA Ops:
  0.0 42.6 %expert_relay.1 = bf16[3,2,7168]{2,1,0:T(2,128)(2,1)} custom-call(bf16[3,2,7168]{2,1,0:T(2,128)(2,1)} %bitcast.6, f32[1,7168]{1,0:T(1,128)} %bitcast.7, s32[2,2,3]{2,1,0:T(2,128)} %bitcast.8, f32[2,2,3]{2,1,0:T(2,128)} %bitcast.9, bf16[1,7168,512]{2,1,0:T(8,128)(2,1)} %w_gate.1, bf16[1,7168,512]{2,1,0:T(8,128)(2,1)} %w_up.1, bf16[1,512,7168]{2,1,0:T(8,128)(2,1)} %w_down.1), custom_call_target="tpu_custom_call" | custom-call | flops 2113929216 | bytes 22020096 | tf_op jit(solution)/shard_map/expert_relay/pallas_call | solution.py:303
  42.6 1.6 %copy.9 = bf16[2,3,7168]{2,0,1:T(2,128)(2,1)} copy(bf16[2,3,7168]{2,0,1:T(2,128)(2,1)} %bitcast.5) | data formatting | bytes 172032

commit v5 on v4

--- a/solution.py
+++ b/solution.py
@@ -20,12 +20,13 @@
     sections, locals_, chunks,
     tokens, gain, routes, gate_weight, w_gate, w_up, w_down,
     out,
-    gate_v, up_v, down_v, wide_rows, packed, rows_in, rows, gate_acc, up_acc, arrived,
+    both_v, down_v, wide_rows, packed, rows_in, rows, acts, arrived,
     own_weights, all_weights, row_weights, packing, spreading, parts, core_in, pair_in, sums, local_in,
     load_sem, a_send, a_recv, w1_send, w1_recv, w2_send, w2_recv,
     s1_send, s1_recv, s2_send, s2_recv, r1_send, r1_recv, r2_send, r2_recv, r3_send, r3_recv,
 ):
     tok, micro, width = tokens.shape
+    hid = down_v.shape[0]
     step = width // chunks
     count = tok * micro
     group = locals_ * count
@@ -56,10 +57,10 @@
         )
 
     def gate_load(k):
-        return pltpu.make_async_copy(w_gate.at[0, cut(k), :], gate_v.at[cut(k), :], load_sem.at[0, k])
+        return pltpu.make_async_copy(w_gate.at[0, cut(k), :], both_v.at[cut(k), 0:hid], load_sem.at[0, k])
 
     def up_load(k):
-        return pltpu.make_async_copy(w_up.at[0, cut(k), :], up_v.at[cut(k), :], load_sem.at[1, k])
+        return pltpu.make_async_copy(w_up.at[0, cut(k), :], both_v.at[cut(k), hid:2 * hid], load_sem.at[1, k])
 
     def down_load(k):
         return pltpu.make_async_copy(w_down.at[0, :, cut(k)], down_v.at[:, cut(k)], load_sem.at[2, k])
@@ -99,7 +100,6 @@
             packing[0, p * count:p * count + BLOCK, :] = wide_rows[:, narrow(k, p)]
         packed[k] = packing[0, 0:pack, :].astype(jnp.bfloat16)
 
-    each(0, chunks, pack_own)
 
     pl.semaphore_wait(barrier, 2 * locals_ + 1)
 
@@ -121,6 +121,7 @@
                  s1_send.at[k, other], s1_recv.at[k, other], (ahead, node, local)).wait_recv()
 
     def s1_start(k):
+        pack_own(k)
         for offset in range(locals_):
             s1(k, offset).start()
 
@@ -132,8 +133,7 @@
         return send(rows.at[block, :, cut(k)], rows.at[block, :, cut(k)],
                     s2_send.at[k, which], s2_recv.at[k, which], (section, to, local))
 
-    gate_acc[...] = jnp.zeros_like(gate_acc)
-    up_acc[...] = jnp.zeros_like(up_acc)
+    acts[...] = jnp.zeros_like(acts)
 
     def w2(which, block, to):
         return send(all_weights.at[block], all_weights.at[block],
@@ -181,13 +181,12 @@
             gate_load(k).wait()
             up_load(k).wait()
             piece = rows[:, :, cut(k)].astype(jnp.float32).reshape(total, step).astype(jnp.bfloat16)
-            gate_acc[...] += jnp.dot(piece, gate_v[cut(k), :], preferred_element_type=jnp.float32)
-            up_acc[...] += jnp.dot(piece, up_v[cut(k), :], preferred_element_type=jnp.float32)
+            acts[...] += jnp.dot(piece, both_v[cut(k), :], preferred_element_type=jnp.float32)
 
     each(0, chunks + FAR_LAG + 1, in_step)
 
-    gate = gate_acc[...]
-    hidden = (gate / (1.0 + jnp.exp(-gate)) * up_acc[...]).astype(jnp.bfloat16)
+    gate = acts[:, 0:hid]
+    hidden = (gate / (1.0 + jnp.exp(-gate)) * acts[:, hid:2 * hid]).astype(jnp.bfloat16)
 
     w2(1, near, near).wait_recv()
     w2(2, cross, near).wait_recv()
@@ -284,7 +283,7 @@
 
     each(0, chunks, last_step)
     for t in range(tok):
-        out[t] = wide_rows[t * micro:(t + 1) * micro, :].astype(jnp.bfloat16)
+        out[t] = wide_rows[t * micro:(t + 1) * micro, :]
 
 
 def shards(sections, nodes, locals_, tokens, norm_gain, routes, gate_weight, w_gate, w_up, w_down):
@@ -302,15 +301,15 @@
     tokens = tokens.transpose(1, 0, 2)
     mixed = pl.pallas_call(
         functools.partial(kernel, sections, locals_, chunks),
-        out_shape=jax.ShapeDtypeStruct(tokens.shape, bf),
+        out_shape=jax.ShapeDtypeStruct(tokens.shape, f32),
         in_specs=[here] * 4 + [away] * 3,
         out_specs=here,
         scratch_shapes=[
-            vmem((width, hid), bf), vmem((width, hid), bf), vmem((hid, width), bf),
+            vmem((width, 2 * hid), bf), vmem((hid, width), bf),
             vmem((BLOCK, width), f32), vmem((chunks, pack, part), bf),
             vmem((chunks, locals_, pack, part), bf),
             vmem((nodes, group, width), bf),
-            vmem((total, hid), f32), vmem((total, hid), f32),
+            vmem((total, 2 * hid), f32),
             vmem(tokens.shape, bf),
             vmem((BLOCK, LANES), f32), vmem((nodes, locals_, BLOCK, LANES), f32),
             vmem((total + BLOCK, LANES), f32),
@@ -337,7 +336,7 @@
         tokens, norm_gain.reshape(1, width), routes.transpose(0, 2, 1), gate_weight.transpose(0, 2, 1),
         w_gate, w_up, w_down,
     )
-    return mixed.transpose(1, 0, 2)
+    return mixed.astype(bf).transpose(1, 0, 2)
 
 
 def solution(mesh):

time: 44.4 us -> 44.5 us (level)
  other arithmetic: 0 us -> 1.62 us
  local copies, waits for them, and re-layouts: 1.59 us -> 0 us
    transpose x0 -> x1, other arithmetic: none -> 1.62 us  [shards(): return mixed.astype(bf).transpose(1, 0, 2)]
    unnamed x1 -> x0, local copies, waits for them, and re-layouts: 1.59 us -> none
where the time goes in v5:
time: 44.5 us; the launch traced here: 44.3 us
  Pallas kernels  42.7 us (96%)
  other arithmetic  1.62 us (4%)
    pallas_call x1, Pallas kernels, shards(): pl.pallas_call(functools.partial(kernel, sections, locals_, chunks), out_...  42.7 us
    transpose x1, other arithmetic, shards(): return mixed.astype(bf).transpose(1, 0, 2)  1.62 us

profile of v5, /device:TPU:0, one launch (start us, length us, event | category | flops | bytes accessed | tf_op | source)
XLA Modules:
  0.0 44.3 jit_solution(7259307047806367661)
XLA Ops:
  0.0 42.7 %expert_relay.1 = f32[3,2,7168]{2,1,0:T(2,128)} custom-call(bf16[3,2,7168]{2,1,0:T(2,128)(2,1)} %bitcast.6, f32[1,7168]{1,0:T(1,128)} %bitcast.7, s32[2,2,3]{2,1,0:T(2,128)} %bitcast.8, f32[2,2,3]{2,1,0:T(2,128)} %bitcast.9, bf16[1,7168,512]{2,1,0:T(8,128)(2,1)} %w_gate.1, bf16[1,7168,512]{2,1,0:T(8,128)(2,1)} %w_up.1, bf16[1,512,7168]{2,1,0:T(8,128)(2,1)} %w_down.1), custom_call_target="tpu_custom_call" | custom-call | flops 2113929216 | bytes 22020096 | tf_op jit(solution)/shard_map/expert_relay/pallas_call | solution.py:302
  42.7 1.6 %convert_bitcast_fusion = bf16[2,3,7168]{2,0,1:T(2,128)(2,1)} fusion(f32[3,2,7168]{2,1,0:T(2,128)} %expert_relay.1), kind=kLoop, calls=%fused_computation | loop fusion | flops 43008 | bytes 258048 | tf_op jit(solution)/shard_map/transpose | solution.py:339

commit v6 on v5

--- a/solution.py
+++ b/solution.py
@@ -14,6 +14,7 @@
 CORE_LAG = 2
 PAIR_LAG = 4
 PIECES = 4
+AHEAD = 3
 
 
 def kernel(
@@ -125,9 +126,8 @@
         for offset in range(locals_):
             s1(k, offset).start()
 
-    each(0, chunks, s1_start)
+    each(0, AHEAD, s1_start)
     carry = send(tokens, arrived, a_send, a_recv, (ahead, node, local))
-    carry.start()
 
     def s2(k, which, block, to):
         return send(rows.at[block, :, cut(k)], rows.at[block, :, cut(k)],
@@ -152,6 +152,14 @@
             rows[node, :, cut(i)] = spreading[0:group, :].astype(jnp.bfloat16)
             s2(i, 0, node, far).start()
             s2(i, 1, node, near).start()
+
+        @pl.when(i < chunks - AHEAD)
+        def _():
+            s1_start(i + AHEAD)
+
+        @pl.when(i == chunks - 1)
+        def _():
+            carry.start()
 
         @pl.when(i == 1)
         def _():

time: 44.5 us -> 44.2 us (level)
  no operation moved by 1% of the time
where the time goes in v6:
time: 44.2 us; the launch traced here: 44.1 us
  Pallas kernels  42.4 us (96%)
  other arithmetic  1.62 us (4%)
    pallas_call x1, Pallas kernels, shards(): pl.pallas_call(functools.partial(kernel, sections, locals_, chunks), out_...  42.4 us
    transpose x1, other arithmetic, shards(): return mixed.astype(bf).transpose(1, 0, 2)  1.62 us

profile of v6, /device:TPU:0, one launch (start us, length us, event | category | flops | bytes accessed | tf_op | source)
XLA Modules:
  0.0 44.1 jit_solution(6512308999696523245)
XLA Ops:
  0.0 42.4 %expert_relay.1 = f32[3,2,7168]{2,1,0:T(2,128)} custom-call(bf16[3,2,7168]{2,1,0:T(2,128)(2,1)} %bitcast.6, f32[1,7168]{1,0:T(1,128)} %bitcast.7, s32[2,2,3]{2,1,0:T(2,128)} %bitcast.8, f32[2,2,3]{2,1,0:T(2,128)} %bitcast.9, bf16[1,7168,512]{2,1,0:T(8,128)(2,1)} %w_gate.1, bf16[1,7168,512]{2,1,0:T(8,128)(2,1)} %w_up.1, bf16[1,512,7168]{2,1,0:T(8,128)(2,1)} %w_down.1), custom_call_target="tpu_custom_call" | custom-call | flops 2113929216 | bytes 22020096 | tf_op jit(solution)/shard_map/expert_relay/pallas_call | solution.py:310
  42.4 1.6 %convert_bitcast_fusion = bf16[2,3,7168]{2,0,1:T(2,128)(2,1)} fusion(f32[3,2,7168]{2,1,0:T(2,128)} %expert_relay.1), kind=kLoop, calls=%fused_computation | loop fusion | flops 43008 | bytes 258048 | tf_op jit(solution)/shard_map/transpose | solution.py:347
